TPU v7x, 128 devices: a whole 4x4x4 slice. The times are simulated.
128 devices in a mesh: dp: 32 (over x, z, core), owner: 4 (over y).
Axes of the slice: x: 4, y: 4, z: 4, core: 2. Of those that a mesh axis runs over, the one named last changes fastest.
Arguments:
- hidden: bfloat16 [32768, 6912], P(('dp', 'owner')), may hold values from -6 to 6
- grad_out: bfloat16 [32768, 2560], P(('dp', 'owner')), may hold values from -6 to 6
- block_list: int32 [512, 2], replicated, may hold values from 0 to 107, as said below
- live_block_count: int32 [128], replicated, may hold values from 1 to 4, as said below
- master: float32 [512, 4096], P(('dp', 'owner')), may hold values from -6 to 6
- moment: float32 [512, 4096], P(('dp', 'owner')), may hold values from -6 to 6
- variance: float32 [512, 4096], P(('dp', 'owner')), may hold values from 0.25 to 4
Outputs:
- new_master: float32 [512, 4096], P(('dp', 'owner'))
- new_moment: float32 [512, 4096], P(('dp', 'owner'))
- new_variance: float32 [512, 4096], P(('dp', 'owner'))
- clipped_grad: float32 [512, 4096], P(('dp', 'owner'))
- published: bfloat16 [512, 4096], replicated
Inputs may be any that keep to these rules, and one draw needn't show every extreme that they name: `block_list`: each row names a block: its row index below 108, its column index below 40; all rows name different blocks. Rows 4 o to 4 o + 3 are owner o's slots; owner o is the device whose index along dp is o // 4 and whose index along the mesh axis `owner` is o mod 4. Owner o's first live_block_count[o] slots are live, the rest padding; some owner's slots are all live.
All inputs are finite; a program needn't handle non-finite values.
Results may differ from a plain program's by a relative error of at most 0.001.
Values may be sent and summed in bfloat16 or wider, within the bound.
A program may use at most 128 MiB of HBM per device.

v0:
```python
import math
import jax
import jax.numpy as jnp
from jax import lax
from jax.sharding import PartitionSpec as P

BLOCK_SIDE_SIZE = 64
OWNER_SLOTS = 4


def block_terms(hidden, grad_out, row_indices, column_indices, active_slot_mask, row_count):
    tok_rows = hidden.shape[0]
    block_side = BLOCK_SIDE_SIZE
    group_size = math.gcd(row_count, 8 * OWNER_SLOTS)
    hidden_blocks = hidden.reshape(tok_rows, hidden.shape[1] // block_side, block_side)
    output_blocks = grad_out.reshape(tok_rows, grad_out.shape[1] // block_side, block_side)

    def one_group(id_pair):
        row_sel, col_sel = id_pair
        left_cols = jnp.take(hidden_blocks, row_sel, axis=1)
        right_cols = jnp.take(output_blocks, col_sel, axis=1)
        products = lax.dot_general(
            left_cols, right_cols, (((0,), (0,)), ((1,), (1,))), preferred_element_type=jnp.float32
        )
        return products.reshape(group_size, block_side * block_side)

    group_terms = lax.map(
        one_group, (row_indices.reshape(-1, group_size), column_indices.reshape(-1, group_size))
    )
    group_terms = group_terms.reshape(row_count, block_side * block_side)
    return jnp.where(active_slot_mask[:, None], group_terms, jnp.zeros_like(group_terms))


def local(hidden, grad_out, block_list, live_block_count, master, moment, variance):
    slot_rows = master.shape[0]
    row_indices = block_list[:, 0]
    column_indices = block_list[:, 1]
    active_slot_mask = (
        jnp.arange(slot_rows, dtype=jnp.int32)[None, :] < live_block_count[:, None]
    ).reshape(-1)
    weight_gradient = lax.psum_scatter(
        block_terms(
            hidden,
            grad_out,
            row_indices,
            column_indices,
            active_slot_mask,
            lax.axis_size(("dp", "owner")) * slot_rows,
        ),
        ("dp", "owner"),
        scatter_dimension=0,
        tiled=True,
    )
    square_total = lax.psum(jnp.sum(weight_gradient * weight_gradient), ("dp", "owner"))
    live_total = jnp.sum(live_block_count).astype(jnp.float32) * weight_gradient.shape[1]
    mean_square = square_total / live_total
    clip_scale = jnp.minimum(1.0, 1.0 / jnp.sqrt(mean_square + 1e-06))
    clipped_grad = clip_scale * weight_gradient
    new_moment = 0.9 * moment + 0.1 * clipped_grad
    new_variance = 0.95 * variance + 0.05 * clipped_grad * clipped_grad
    moment_hat = new_moment / (1.0 - 0.9**20)
    variance_hat = new_variance / (1.0 - 0.95**20)
    new_master = master - 0.02 * (moment_hat / (jnp.sqrt(variance_hat) + 1e-08) + 0.1 * master)
    own_blocks = new_master.astype(jnp.bfloat16)
    published = lax.all_gather(own_blocks, ("dp", "owner"), axis=0, tiled=True)
    return (new_master, new_moment, new_variance, clipped_grad, published)


def solution(mesh):
    return jax.shard_map(
        local,
        mesh=mesh,
        in_specs=(
            P(("dp", "owner"), None),
            P(("dp", "owner"), None),
            P(),
            P(),
            P(("dp", "owner"), None),
            P(("dp", "owner"), None),
            P(("dp", "owner"), None),
        ),
        out_specs=(
            P(("dp", "owner"), None),
            P(("dp", "owner"), None),
            P(("dp", "owner"), None),
            P(("dp", "owner"), None),
            P(),
        ),
        check_vma=False,
    )
```

profile of v0, /device:TPU:1, one launch (start us, length us, event | category | flops | bytes accessed | tf_op | source)
XLA Modules:
  0.0 451.4 jit_solution(7616821432423559366)
XLA Ops:
  8.2 6.0 %copy.16 = bf16[256,6912]{0,1:T(8,128)(2,1)} copy(bf16[256,6912]{1,0:T(8,128)(2,1)} %param.9) | data formatting | bytes 7077888 | tf_op args[0]
  14.1 1.6 copy.17
  15.7 115.8 %while.10 = (s32[]{:T(128)}, f32[16,32,4096]{2,1,0:T(8,128)}, s32[16,32]{1,0:T(8,128)S(1)}, bf16[256,108,64]{0,2,1:T(8,128)(2,1)}, s32[16,32]{1,0:T(8,128)S(1)}, /*index=5*/bf16[256,40,64]{0,2,1:T(8,128)(2,1)S(1)}, s32[]{:T(128)}) while((s32[]{:T(128)}, f32[16,32,4096]{2,1,0:T(8,128)}, s32[16,32]{1,0:T(8,128)S(1)}, ...), condition=%wide.region_1.2_spmd, body=%wide.region_0.1_spmd.sunk | while | flops 68160064 | bytes 8923093 | solution.py:27
  16.4 2.6 gather_fusion.1
  20.6 1.6 broadcast_in_dim.44
  23.7 2.6 gather_fusion.1
  27.8 1.6 broadcast_in_dim.44
  31.0 2.6 gather_fusion.1
  35.1 1.6 broadcast_in_dim.44
  38.2 2.6 gather_fusion.1
  42.4 1.6 broadcast_in_dim.44
  45.4 2.6 gather_fusion.1
  48.1 1.5 fusion.20
  49.6 1.6 broadcast_in_dim.44
  52.7 2.6 gather_fusion.1
  56.8 1.6 broadcast_in_dim.44
  59.9 2.6 gather_fusion.1
  64.1 1.6 broadcast_in_dim.44
  67.1 2.6 gather_fusion.1
  71.3 1.6 broadcast_in_dim.44
  74.4 2.6 gather_fusion.1
  77.0 1.5 fusion.20
  78.5 1.6 broadcast_in_dim.44
  81.6 2.6 gather_fusion.1
  84.3 1.5 fusion.20
  85.8 1.6 broadcast_in_dim.44
  88.9 2.6 gather_fusion.1
  91.5 1.5 fusion.20
  93.0 1.6 broadcast_in_dim.44
  96.1 2.6 gather_fusion.1
  100.2 1.6 broadcast_in_dim.44
  103.3 2.6 gather_fusion.1
  107.5 1.6 broadcast_in_dim.44
  110.5 2.6 gather_fusion.1
  113.2 1.5 fusion.20
  114.7 1.6 broadcast_in_dim.44
  117.8 2.6 gather_fusion.1
  120.4 1.5 fusion.20
  121.9 1.6 broadcast_in_dim.44
  125.0 2.6 gather_fusion.1
  129.1 1.6 broadcast_in_dim.44
  131.8 8.2 %bitcast_select_fusion = f32[512,4096]{1,0:T(8,128)} fusion(f32[16,32,4096]{2,1,0:T(8,128)} %get-tuple-element.37, pred[512]{0:T(512)(128)(4,1)S(1)} %lt.64), kind=kLoop, calls=%fused_computation.24 | loop fusion | flops 2097152 | bytes 16777728 | tf_op jit(solution)/shard_map/jit(_where)/select_n | solution.py:31
  141.4 163.7 %all-reduce.3.cloned.1.call-done = f32[512,4096]{1,0:T(8,128)} async-done(((f32[512,4096]{1,0:T(8,128)}), f32[512,4096]{1,0:T(8,128)}) %all-reduce.3.cloned.1.call-update) | async-done | bytes 8388624
  305.1 1.5 multiply_reduce_fusion
  306.7 64.0 %psum.7 = f32[]{:T(128)} all-reduce(f32[]{:T(128)} %multiply_reduce_fusion), channel_id=1, replica_groups=mesh['dp'=32,'owner'=4] {'dp','owner'}, use_global_device_ids=true, to_apply=%region_4.5 | all-reduce | flops 1 | bytes 8 | tf_op jit(solution)/shard_map/psum | solution.py:54
  371.4 1.7 convert_bitcast_fusion
  373.1 64.5 %all-gather.3.cloned.1.call-done = bf16[128,4,4096]{2,1,0:T(4,128)(2,1)} async-done(((bf16[1,4,4096]{2,1,0:T(4,128)(2,1)}), bf16[128,4,4096]{2,1,0:T(4,128)(2,1)}) %all-gather.3.cloned.1.call-update) | async-done | bytes 4194320 | tf_op jit(solution)/shard_map/all_gather | solution.py:65
  437.7 6.9 %reshape.124 = bf16[512,4096]{1,0:T(8,128)(2,1)} reshape(bf16[128,4,4096]{2,1,0:T(4,128)(2,1)} %all-gather.3.cloned.1.call-done) | data formatting | bytes 8388608
  (125 shorter events, 41.0 us)
Async XLA Ops:
  7.2 298.0 %all-reduce.3.cloned.1.call-start = ((), (), s32[]{:S(2)}) async-start(), calls=%async_computation.1 | async-start | bytes 16777216
  15.7 115.8 %copy-start.3 = (s32[128]{0:T(128)S(1)}, s32[128]{0:T(128)}, u32[]{:S(2)}) copy-start(s32[128]{0:T(128)} %param.12) | copy-start | bytes 1540
  140.0 231.4 %copy-start = (f32[4,4096]{1,0:T(4,128)S(1)}, f32[4,4096]{1,0:T(4,128)}, u32[]{:S(2)}) copy-start(f32[4,4096]{1,0:T(4,128)} %param.13) | copy-start | bytes 196612
  140.0 231.4 %copy-start.1 = (f32[4,4096]{1,0:T(4,128)S(1)}, f32[4,4096]{1,0:T(4,128)}, u32[]{:S(2)}) copy-start(f32[4,4096]{1,0:T(4,128)} %param.14) | copy-start | bytes 196612
  140.0 231.4 %copy-start.2 = (f32[4,4096]{1,0:T(4,128)S(1)}, f32[4,4096]{1,0:T(4,128)}, u32[]{:S(2)}) copy-start(f32[4,4096]{1,0:T(4,128)} %param.15) | copy-start | bytes 196612
  140.0 297.6 %all-gather.3.cloned.1.call-start = ((), (), s32[]{:S(2)}) async-start(), calls=%async_computation | async-start | bytes 4227072 | tf_op jit(solution)/shard_map/all_gather | solution.py:65
Sparse Core Ops, SparseCore 0:
  140.2 164.9 all-reduce.2
  373.3 64.3 all-gather.2
where the time goes:
time: 453 us; the launch traced here: 451 us
  waiting for transfers between devices  228 us (50%)
  local copies, waits for them, and re-layouts  106 us (23%)
  blocking collectives  64 us (14%)
  matrix products  24 us (5%)
  between operations  15.5 us (3%)
  other arithmetic  12.8 us (3%)
    unnamed x3, waiting for transfers between devices  164 us
    all_gather x1, waiting for transfers between devices, local(): published = lax.all_gather(own_blocks, ('dp', 'owner'), axis=0, tiled=True)  64.5 us
    psum x1, blocking collectives, local(): lax.psum(jnp.sum(weight_gradient * weight_gradient), ('dp', 'owner'))  64 us
    gather x16, local copies, waits for them, and re-layouts, one_group(): left_cols = jnp.take(hidden_blocks, row_sel, axis=1)  41.9 us
    broadcast_in_dim x16, local copies, waits for them, and re-layouts, block_terms(): lax.map(one_group, (row_indices.reshape(-1, group_size), column_indices.r...  25.3 us
    dot_general x16, matrix products, one_group(): lax.dot_general(left_cols, right_cols, (((0,), (0,)), ((1,), (1,))), pref...  24 us
    unnamed x11, local copies, waits for them, and re-layouts  14.5 us
    dynamic_update_slice x16, local copies, waits for them, and re-layouts, block_terms(): lax.map(one_group, (row_indices.reshape(-1, group_size), column_indices.r...  13.6 us
  transfers between devices with their start and end apart: 2, of which 2 were waited for; matrix products, arithmetic and copies ran while one was open for 0% of the time, Pallas kernels for 0%

commit v1 on v0

--- a/solution.py
+++ b/solution.py
@@ -62,7 +62,12 @@
     variance_hat = new_variance / (1.0 - 0.95**20)
     new_master = master - 0.02 * (moment_hat / (jnp.sqrt(variance_hat) + 1e-08) + 0.1 * master)
     own_blocks = new_master.astype(jnp.bfloat16)
-    published = lax.all_gather(own_blocks, ("dp", "owner"), axis=0, tiled=True)
+    published = jnp.concatenate(
+        lax.all_to_all(
+            jnp.stack([own_blocks] * lax.axis_size(("dp", "owner"))), ("dp", "owner"), 0, 0
+        ),
+        axis=0,
+    )
     return (new_master, new_moment, new_variance, clipped_grad, published)
 
 

time: 453 us -> 449 us (level)
  waiting for transfers between devices: 228 us -> 164 us
  blocking collectives: 64 us -> 123 us
    all_gather x1 -> x0, waiting for transfers between devices: 64.5 us -> none  [local(): published = lax.all_gather(own_blocks, ('dp', 'owner'), axis=0, tiled=True)]
    all_to_all x0 -> x1, blocking collectives: none -> 58.7 us  [local(): lax.all_to_all(jnp.stack([own_blocks] * lax.axis_size(('dp', 'owner'))),...]
    reshape x0 -> x1, local copies, waits for them, and re-layouts: none -> 6.87 us  [local(): jnp.concatenate(lax.all_to_all(jnp.stack([own_blocks] * lax.axis_size(('d...]
    unnamed x11 -> x10, local copies, waits for them, and re-layouts: 14.5 us -> 7.59 us
    unnamed x3 -> x2, waiting for transfers between devices: 164 us -> 164 us
  transfers between devices with their start and end apart: 2 -> 1, of which waited for: 2 -> 1; matrix products, arithmetic and copies ran while one was open for 0% -> 0% of each run, Pallas kernels for 0% -> 0%
where the time goes in v1:
time: 449 us; the launch traced here: 448 us
  waiting for transfers between devices  164 us (37%)
  blocking collectives  123 us (27%)
  local copies, waits for them, and re-layouts  108 us (24%)
  matrix products  24 us (5%)
  between operations  15.5 us (3%)
  other arithmetic  12.8 us (3%)
    unnamed x2, waiting for transfers between devices  164 us
    psum x1, blocking collectives, local(): lax.psum(jnp.sum(weight_gradient * weight_gradient), ('dp', 'owner'))  64 us
    all_to_all x1, blocking collectives, local(): lax.all_to_all(jnp.stack([own_blocks] * lax.axis_size(('dp', 'owner'))),...  58.7 us
    gather x16, local copies, waits for them, and re-layouts, one_group(): left_cols = jnp.take(hidden_blocks, row_sel, axis=1)  41.9 us
    broadcast_in_dim x16, local copies, waits for them, and re-layouts, block_terms(): lax.map(one_group, (row_indices.reshape(-1, group_size), column_indices.r...  25.3 us
    dot_general x16, matrix products, one_group(): lax.dot_general(left_cols, right_cols, (((0,), (0,)), ((1,), (1,))), pref...  24 us
    dynamic_update_slice x16, local copies, waits for them, and re-layouts, block_terms(): lax.map(one_group, (row_indices.reshape(-1, group_size), column_indices.r...  13.6 us
    gather x16, local copies, waits for them, and re-layouts, one_group(): right_cols = jnp.take(output_blocks, col_sel, axis=1)  9.82 us
  transfers between devices with their start and end apart: 1, of which 1 were waited for; matrix products, arithmetic and copies ran while one was open for 0% of the time, Pallas kernels for 0%

profile of v1, /device:TPU:1, one launch (start us, length us, event | category | flops | bytes accessed | tf_op | source)
XLA Modules:
  0.0 447.6 jit_solution(15638497430426440236)
XLA Ops:
  8.2 6.0 %copy.16 = bf16[256,6912]{0,1:T(8,128)(2,1)} copy(bf16[256,6912]{1,0:T(8,128)(2,1)} %param.9) | data formatting | bytes 7077888 | tf_op args[0]
  14.1 1.6 copy.17
  15.7 115.8 %while.10 = (s32[]{:T(128)}, f32[16,32,4096]{2,1,0:T(8,128)}, s32[16,32]{1,0:T(8,128)S(1)}, bf16[256,108,64]{0,2,1:T(8,128)(2,1)}, s32[16,32]{1,0:T(8,128)S(1)}, /*index=5*/bf16[256,40,64]{0,2,1:T(8,128)(2,1)S(1)}, s32[]{:T(128)}) while((s32[]{:T(128)}, f32[16,32,4096]{2,1,0:T(8,128)}, s32[16,32]{1,0:T(8,128)S(1)}, ...), condition=%wide.region_1.2_spmd, body=%wide.region_0.1_spmd.sunk | while | flops 68160064 | bytes 8923093 | solution.py:27
  16.4 2.6 gather_fusion.1
  20.6 1.6 broadcast_in_dim.44
  23.7 2.6 gather_fusion.1
  27.8 1.6 broadcast_in_dim.44
  31.0 2.6 gather_fusion.1
  35.1 1.6 broadcast_in_dim.44
  38.2 2.6 gather_fusion.1
  42.4 1.6 broadcast_in_dim.44
  45.4 2.6 gather_fusion.1
  48.1 1.5 fusion.21
  49.6 1.6 broadcast_in_dim.44
  52.7 2.6 gather_fusion.1
  56.8 1.6 broadcast_in_dim.44
  59.9 2.6 gather_fusion.1
  64.1 1.6 broadcast_in_dim.44
  67.1 2.6 gather_fusion.1
  71.3 1.6 broadcast_in_dim.44
  74.4 2.6 gather_fusion.1
  77.0 1.5 fusion.21
  78.5 1.6 broadcast_in_dim.44
  81.6 2.6 gather_fusion.1
  84.3 1.5 fusion.21
  85.8 1.6 broadcast_in_dim.44
  88.9 2.6 gather_fusion.1
  91.5 1.5 fusion.21
  93.0 1.6 broadcast_in_dim.44
  96.1 2.6 gather_fusion.1
  100.2 1.6 broadcast_in_dim.44
  103.3 2.6 gather_fusion.1
  107.5 1.6 broadcast_in_dim.44
  110.5 2.6 gather_fusion.1
  113.2 1.5 fusion.21
  114.7 1.6 broadcast_in_dim.44
  117.8 2.6 gather_fusion.1
  121.9 1.6 broadcast_in_dim.44
  125.0 2.6 gather_fusion.1
  129.1 1.6 broadcast_in_dim.44
  131.8 8.2 %bitcast_select_fusion = f32[512,4096]{1,0:T(8,128)} fusion(f32[16,32,4096]{2,1,0:T(8,128)} %get-tuple-element.37, pred[512]{0:T(512)(128)(4,1)S(1)} %lt.64), kind=kLoop, calls=%fused_computation.24 | loop fusion | flops 2097152 | bytes 16777728 | tf_op jit(solution)/shard_map/jit(_where)/select_n | solution.py:31
  141.3 163.8 %all-reduce.3.cloned.1.call-done = f32[512,4096]{1,0:T(8,128)} async-done(((f32[512,4096]{1,0:T(8,128)}), f32[512,4096]{1,0:T(8,128)}) %all-reduce.3.cloned.1.call-update) | async-done | bytes 8388624
  305.1 1.5 multiply_reduce_fusion
  306.7 64.0 %psum.7 = f32[]{:T(128)} all-reduce(f32[]{:T(128)} %multiply_reduce_fusion), channel_id=1, replica_groups=mesh['dp'=32,'owner'=4] {'dp','owner'}, use_global_device_ids=true, to_apply=%region_4.5 | all-reduce | flops 1 | bytes 8 | tf_op jit(solution)/shard_map/psum | solution.py:54
  371.4 1.7 fusion.12
  373.1 2.1 stack.2
  375.2 58.7 %all_to_all.5 = bf16[128,4,4096]{2,1,0:T(4,128)(2,1)} all-to-all(bf16[128,4,4096]{2,1,0:T(4,128)(2,1)S(1)} %stack.2), channel_id=1, replica_groups=mesh['dp'=32,'owner'=4] {'dp','owner'}, dimensions={0} | all-to-all | bytes 8388608 | tf_op jit(solution)/shard_map/all_to_all | solution.py:66
  433.9 6.9 %reshape.112 = bf16[512,4096]{1,0:T(8,128)(2,1)} reshape(bf16[128,4,4096]{2,1,0:T(4,128)(2,1)} %all_to_all.5) | data formatting | bytes 8388608 | tf_op jit(solution)/shard_map/reshape | solution.py:65
  (124 shorter events, 42.4 us)
Async XLA Ops:
  7.2 298.0 %all-reduce.3.cloned.1.call-start = ((), (), s32[]{:S(2)}) async-start(), calls=%async_computation.1 | async-start | bytes 16777216
  15.7 115.8 %copy-start.3 = (s32[128]{0:T(128)S(1)}, s32[128]{0:T(128)}, u32[]{:S(2)}) copy-start(s32[128]{0:T(128)} %param.12) | copy-start | bytes 1540
  140.0 231.4 %copy-start = (f32[4,4096]{1,0:T(4,128)S(1)}, f32[4,4096]{1,0:T(4,128)}, u32[]{:S(2)}) copy-start(f32[4,4096]{1,0:T(4,128)} %param.13) | copy-start | bytes 196612
  140.0 231.4 %copy-start.1 = (f32[4,4096]{1,0:T(4,128)S(1)}, f32[4,4096]{1,0:T(4,128)}, u32[]{:S(2)}) copy-start(f32[4,4096]{1,0:T(4,128)} %param.14) | copy-start | bytes 196612
  140.0 231.4 %copy-start.2 = (f32[4,4096]{1,0:T(4,128)S(1)}, f32[4,4096]{1,0:T(4,128)}, u32[]{:S(2)}) copy-start(f32[4,4096]{1,0:T(4,128)} %param.15) | copy-start | bytes 196612
Sparse Core Ops, SparseCore 0:
  140.2 164.9 all-reduce.2
